TPU v7x, 128 devices: a whole 4x4x4 slice. The times are simulated.
128 devices in a mesh: expert: 8 (over y, z_hi), tp: 16 (over x, z_lo, core).
Axes of the slice: x: 4, y: 4, z: 4 (z_hi: 2, z_lo: 2; z = z_hi * 2 + z_lo), core: 2. Of those that a mesh axis runs over, the one named last changes fastest.
Arguments:
- tokens: bfloat16 [2048, 3072], P(('expert', 'tp')), may hold values from -6 to 6
- routes: int32 [2048, 2], P(('expert', 'tp')), may hold values from 0 to 7, as said below
- counts: int32 [8], replicated, may hold values from 1 to 1536, as said below
- gate_weight: bfloat16 [8, 3072, 8192], P('expert', None, 'tp'), may hold values from -0.109375 to 0.109375
- up_weight: bfloat16 [8, 3072, 8192], P('expert', None, 'tp'), may hold values from -0.109375 to 0.109375
Outputs:
- hessian: float32 [8, 8192, 8192], P('expert', 'tp')
Inputs may be any that keep to these rules, and one draw needn't show every extreme that they name: `routes`: each row names two different experts. Among the 16 rows of one device no expert is named by more than 12 rows, and the same expert is named by exactly 12 rows on every device. counts[e] is the number of rows of routes that name expert e.
All inputs are finite; a program needn't handle non-finite values.
Results may differ from a plain program's by a relative error of at most 0.004.
Values may be sent and summed in bfloat16 or wider, within the bound.
No kernel may reach another device: no remote copies, remote signals or barrier semaphores. Data moves between devices by JAX's collectives and lax.ppermute only.
A program may use at most 128 MiB of HBM per device.

v0:
```python
import jax
import jax.numpy as jnp
from jax import lax
from jax.sharding import PartitionSpec as P


def gram_block(left_panel, right_panel):
    return lax.dot_general(
        left_panel, right_panel, (((0,), (0,)), ((), ())), preferred_element_type=jnp.float32
    )


def local(tokens, routes, counts, gate_weight, up_weight):
    groups = lax.axis_size("expert")
    slot_count = 3 * tokens.shape[0] // 4
    experts = jnp.arange(groups, dtype=jnp.int32)
    named_rows = jnp.sum((routes[:, :, None] == experts[None, None, :]).astype(jnp.int32), axis=1)
    before = jnp.cumsum(named_rows, axis=0) - named_rows
    places = jnp.arange(slot_count, dtype=jnp.int32)
    slot_picks = named_rows[:, :, None] * (before[:, :, None] == places[None, None, :]).astype(
        jnp.int32
    )
    placing = (
        jnp.transpose(slot_picks, (1, 2, 0))
        .reshape(groups * slot_count, tokens.shape[0])
        .astype(jnp.bfloat16)
    )
    outgoing = jnp.dot(placing, tokens, preferred_element_type=jnp.float32).astype(jnp.bfloat16)
    outgoing = outgoing.reshape(groups, slot_count, tokens.shape[1])
    arrived = lax.all_to_all(outgoing, "expert", split_axis=0, concat_axis=0, tiled=True)
    arrived = arrived.reshape(groups * slot_count, tokens.shape[1])
    gate_panel = gate_weight[0]
    up_panel = up_weight[0]
    rows_piece = lax.all_gather(arrived, "tp", axis=0, tiled=True)
    gate_part = jnp.dot(rows_piece, gate_panel, preferred_element_type=jnp.float32)
    up_part = jnp.dot(rows_piece, up_panel, preferred_element_type=jnp.float32)
    hidden = (jax.nn.silu(gate_part) * up_part).astype(jnp.bfloat16)
    gram = gram_block(hidden, lax.all_gather(hidden, "tp", axis=1, tiled=True))
    routed_total = jnp.sum(jnp.where(experts == lax.axis_index("expert"), counts, 0)).astype(
        jnp.float32
    )
    return (gram * (2.0 / routed_total))[None]


def solution(mesh):
    in_specs = (
        P(("expert", "tp"), None),
        P(("expert", "tp"), None),
        P(),
        P("expert", None, "tp"),
        P("expert", None, "tp"),
    )
    out_specs = P("expert", "tp", None)
    return jax.shard_map(local, mesh=mesh, in_specs=in_specs, out_specs=out_specs, check_vma=False)
```

profile of v0, /device:TPU:1, one launch (start us, length us, event | category | flops | bytes accessed | tf_op | source)
XLA Modules:
  0.0 268.2 jit_solution(12821946492957605274)
XLA Ops:
  6.5 0.0 copy-start
  6.5 0.0 all-gather.3.cloned.1.call-start
  6.5 0.8 convert_reduce_fusion
  7.4 0.1 copy.10
  7.5 0.1 eq.46
  7.6 0.1 eq.43
  7.7 0.1 eq.44
  7.7 0.1 mul.23
  7.8 0.1 mul.24
  7.9 2.0 convolution_convert_fusion
  10.0 2.1 reshape.21
  12.0 20.8 %all_to_all.5 = bf16[8,12,3072]{2,1,0:T(8,128)(2,1)} all-to-all(bf16[8,12,3072]{2,1,0:T(8,128)(2,1)} %reshape.21), channel_id=1, replica_groups=mesh['expert'=8,'tp'=16] {'expert'}, dimensions={0} | all-to-all | bytes 1179648 | tf_op jit(solution)/shard_map/all_to_all | solution.py:30
  32.9 2.1 reshape.22
  35.0 0.0 all-gather.3.cloned.1.call-update
  35.0 0.0 all-gather.5.cloned.1.call-start
  35.0 57.3 %all-gather.3.cloned.1.call-done = bf16[1536,3072]{1,0:T(8,128)(2,1)} async-done(((bf16[96,3072]{1,0:T(8,128)(2,1)}), bf16[1536,3072]{1,0:T(8,128)(2,1)}) %all-gather.3.cloned.1.call-update) | async-done | bytes 9437200 | tf_op jit(solution)/shard_map/all_gather | solution.py:34
  92.3 0.0 copy-done
  92.3 8.5 %fusion.1 = f32[1536,512]{1,0:T(8,128)S(1)} fusion(bf16[1536,3072]{1,0:T(8,128)(2,1)} %all-gather.3.cloned.1.call-done, bf16[1,3072,512]{2,1,0:T(8,128)(2,1)S(1)} %copy-done), kind=kOutput, calls=%fused_computation.4 | convolution fusion | flops 4831838208 | bytes 15728640 | tf_op jit(solution)/shard_map/dot_general | solution.py:35
  100.8 0.0 copy-start.3
  100.8 6.5 %fusion.3 = bf16[1536,512]{1,0:T(8,128)(2,1)} fusion(bf16[1536,3072]{1,0:T(8,128)(2,1)S(1)} %copy-done.1, bf16[1,3072,512]{2,1,0:T(8,128)(2,1)S(1)} %copy-done.2, f32[1536,512]{1,0:T(8,128)S(1)} %fusion.1), kind=kOutput, calls=%fused_computation.6 | convolution fusion | flops 4836556800 | bytes 17301504 | tf_op jit(solution)/shard_map/dot_general | solution.py:36
  107.3 0.0 all-gather.5.cloned.1.call-update
  107.3 0.6 fusion.8
  108.6 130.7 %all-gather.5.cloned.1.call-done = bf16[1536,8192]{1,0:T(8,128)(2,1)} async-done(((bf16[1536,512]{1,0:T(8,128)(2,1)}), bf16[1536,8192]{1,0:T(8,128)(2,1)}) %all-gather.5.cloned.1.call-update) | async-done | bytes 25165840 | tf_op jit(solution)/shard_map/all_gather | solution.py:38
  239.4 22.0 %multiply_bitcast_fusion = f32[1,512,8192]{2,1,0:T(8,128)} fusion(bf16[1536,512]{1,0:T(8,128)(2,1)} %fusion.3, bf16[1536,8192]{1,0:T(8,128)(2,1)} %all-gather.5.cloned.1.call-done, f32[]{:T(128)S(6)} %div.8), kind=kOutput, calls=%fused_computation | convolution fusion | flops 12889096192 | bytes 43515908 | tf_op jit(solution)/shard_map/dot_general | solution.py:8
  (8 shorter events, 0.1 us)
Async XLA Ops:
  6.5 85.8 %copy-start = (bf16[1,3072,512]{2,1,0:T(8,128)(2,1)S(1)}, bf16[1,3072,512]{2,1,0:T(8,128)(2,1)}, u32[]{:S(2)}) copy-start(bf16[1,3072,512]{2,1,0:T(8,128)(2,1)} %param.8) | copy-start | bytes 9437188
  6.5 85.8 %all-gather.3.cloned.1.call-start = ((), (), s32[]{:S(2)}) async-start(), calls=%async_computation.1 | async-start | bytes 10027008 | tf_op jit(solution)/shard_map/all_gather | solution.py:34
  35.0 204.4 %all-gather.5.cloned.1.call-start = ((), (), s32[]{:S(2)}) async-start(), calls=%async_computation.2 | async-start | bytes 26738688 | tf_op jit(solution)/shard_map/all_gather | solution.py:38
  92.3 8.5 %copy-start.1 = (bf16[1536,3072]{1,0:T(8,128)(2,1)S(1)}, bf16[1536,3072]{1,0:T(8,128)(2,1)}, u32[]{:S(2)}) copy-start(bf16[1536,3072]{1,0:T(8,128)(2,1)} %all-gather.3.cloned.1.call-done) | copy-start | bytes 28311556
  92.3 8.5 %copy-start.2 = (bf16[1,3072,512]{2,1,0:T(8,128)(2,1)S(1)}, bf16[1,3072,512]{2,1,0:T(8,128)(2,1)}, u32[]{:S(2)}) copy-start(bf16[1,3072,512]{2,1,0:T(8,128)(2,1)} %param.9) | copy-start | bytes 9437188
  100.8 6.5 %copy-start.3 = (s32[8]{0:T(128)S(1)}, s32[8]{0:T(128)}, u32[]{:S(2)}) copy-start(s32[8]{0:T(128)} %param.7) | copy-start | bytes 100
Sparse Core Ops, SparseCore 0:
  35.1 57.1 all-gather.2
  107.4 131.9 all-gather.4
where the time goes:
time: 268 us
  waiting for transfers between devices  188 us (70%)
  matrix products  39 us (15%)
  blocking collectives  20.8 us (8%)
  between operations  14.1 us (5%)
  local copies, waits for them, and re-layouts  4.67 us (2%)
    all_gather x1, waiting for transfers between devices, local(): gram = gram_block(hidden, lax.all_gather(hidden, 'tp', axis=1, tiled=True))  131 us
    all_gather x1, waiting for transfers between devices, local(): rows_piece = lax.all_gather(arrived, 'tp', axis=0, tiled=True)  57.3 us
    dot_general x1, matrix products, gram_block(): lax.dot_general(left_panel, right_panel, (((0,), (0,)), ((), ())), prefer...  22 us
    all_to_all x1, blocking collectives, local(): lax.all_to_all(outgoing, 'expert', split_axis=0, concat_axis=0, tiled=True)  20.8 us
    dot_general x1, matrix products, local(): jnp.dot(rows_piece, gate_panel, preferred_element_type=jnp.float32)  8.46 us
    dot_general x1, matrix products, local(): up_part = jnp.dot(rows_piece, up_panel, preferred_element_type=jnp.float32)  6.47 us
  transfers between devices with their start and end apart: 2, of which 2 were waited for; matrix products, arithmetic and copies ran while one was open for 0% of the time, Pallas kernels for 0%

commit v1 on v0

v1 whole, which is shorter than its diff:
```python
import functools

import jax
import jax.numpy as jnp
from jax import lax
from jax.experimental import pallas as pl
from jax.experimental.pallas import tpu as pltpu
from jax.sharding import Mesh
from jax.sharding import PartitionSpec as P

AXES = ("y", "h", "x", "l", "c")
ROUTE_LANES = 128
VMEM_BYTES = 56 * 1024 * 1024
INTERPRET = False


def ring_hop(a, axis):
    pairs = [(2 * i + c, 2 * ((i + (1, 3)[c]) % 4) + c) for i in range(4) for c in range(2)]
    return lax.ppermute(a, (axis, "c"), pairs)


def swap(a, axis):
    return lax.ppermute(a, axis, [(0, 1), (1, 0)])


def far_swap(a):
    return lax.ppermute(a, ("h", "l"), [(0, 3), (3, 0), (1, 2), (2, 1)])


def ffn_kernel(slots, width, n, expert_ref, base_ref, wg_ref, wu_ref, *rest):
    sources = rest[: 2 * n]
    out_ref, held, rows, sems = rest[2 * n :]
    copies = [
        pltpu.make_async_copy(sources[i], held.at[i], sems.at[i]) for i in range(2 * n)
    ]
    for copy in copies:
        copy.start()
    tokens = held.shape[1]
    block_rows = rows.shape[0] // n
    expert = expert_ref[0].astype(jnp.float32)
    per_device = 16
    first = lax.broadcasted_iota(jnp.int32, (tokens, tokens), 0)
    second = lax.broadcasted_iota(jnp.int32, (tokens, tokens), 1)
    earlier = jnp.logical_and(first // per_device == second // per_device, first < second)
    earlier = earlier.astype(jnp.float32).astype(jnp.bfloat16)
    lane = lax.broadcasted_iota(jnp.int32, (tokens, ROUTE_LANES), 1)
    places = lax.broadcasted_iota(jnp.int32, (block_rows, tokens), 0).astype(jnp.float32)
    ones = jnp.ones((16, ROUTE_LANES), jnp.bfloat16)
    for i in range(n):
        total = None
        for part in range(2):
            j = 2 * i + part
            copies[j].wait()
            named = held[j, :, width:].astype(jnp.float32) == expert
            named = jnp.logical_and(named, lane < 2).astype(jnp.float32).astype(jnp.bfloat16)
            named = lax.dot_general(
                ones, named, (((1,), (1,)), ((), ())), preferred_element_type=jnp.float32
            )
            rank = jnp.dot(
                named.astype(jnp.bfloat16), earlier, preferred_element_type=jnp.float32
            )
            place = base_ref[j, 0:1, :] + rank[0:1, :]
            place = jnp.where(named[0:1, :] > 0.5, place, -1.0)
            pick = (places == place).astype(jnp.float32).astype(jnp.bfloat16)
            got = jnp.dot(pick, held[j, :, :width], preferred_element_type=jnp.float32)
            total = got if total is None else total + got
        rows[i * block_rows : (i + 1) * block_rows, :] = total.astype(jnp.bfloat16)
    gate = jnp.dot(rows[...], wg_ref[...], preferred_element_type=jnp.float32)
    up = jnp.dot(rows[...], wu_ref[...], preferred_element_type=jnp.float32)
    out_ref[...] = (gate / (1.0 + jnp.exp(-gate)) * up).astype(jnp.bfloat16)


def ffn(expert, arrivals, wg, wu):
    n = len(arrivals) // 2
    width, panel = wg.shape
    tokens = arrivals[0][0].shape[0]
    slots = 3 * 16 // 4
    block_rows = 2 * slots * tokens // 16
    bases = jnp.stack([b for _, b in arrivals])
    return pl.pallas_call(
        functools.partial(ffn_kernel, slots, width, n),
        out_shape=jax.ShapeDtypeStruct((n * block_rows, panel), jnp.bfloat16),
        in_specs=[
            pl.BlockSpec(memory_space=pltpu.SMEM),
            pl.BlockSpec(memory_space=pltpu.VMEM),
            pl.BlockSpec(memory_space=pltpu.VMEM),
            pl.BlockSpec(memory_space=pltpu.VMEM),
        ]
        + [pl.BlockSpec(memory_space=pl.ANY)] * (2 * n),
        out_specs=pl.BlockSpec(memory_space=pltpu.VMEM),
        scratch_shapes=[
            pltpu.VMEM((2 * n,) + arrivals[0][0].shape, jnp.bfloat16),
            pltpu.VMEM((n * block_rows, width), jnp.bfloat16),
            pltpu.SemaphoreType.DMA((2 * n,)),
        ],
        compiler_params=pltpu.CompilerParams(vmem_limit_bytes=VMEM_BYTES),
        cost_estimate=pl.CostEstimate(
            flops=4 * n * block_rows * width * panel, bytes_accessed=6_300_000, transcendentals=0
        ),
        interpret=INTERPRET,
    )(expert, bases, wg, wu, *[a for a, _ in arrivals])


def gram_kernel(counts_of, n_chunks, adding, ids_ref, scale_ref, *rest):
    n_sets = len(counts_of)
    own_refs = rest[:n_chunks]
    panel_refs = rest[n_chunks : n_chunks * (1 + n_sets)]
    old_ref = rest[n_chunks * (1 + n_sets)] if adding else None
    out_ref, turned = rest[-1 - n_chunks], rest[-n_chunks:]
    step = pl.program_id(0)

    @pl.when(step == 0)
    def _():
        for k in range(n_chunks):
            turned[k][...] = own_refs[k][...].T

    start = 0
    for s, count in enumerate(counts_of):

        @pl.when(jnp.logical_and(step >= start, step < start + count))
        def _(s=s):
            total = None
            for k in range(n_chunks):
                part = jnp.dot(
                    turned[k][...],
                    panel_refs[k * n_sets + s][0],
                    preferred_element_type=jnp.float32,
                )
                total = part if total is None else total + part
            total = total * scale_ref[0]
            out_ref[...] = total + old_ref[...] if adding else total

        start += count


def gram(ids, scale, owns, panels, features, old=None):
    counts_of = [p.shape[0] for p in panels[0]]
    panel = owns[0].shape[1]
    starts = [sum(counts_of[:s]) for s in range(len(counts_of))]
    specs, args = [], []
    for own in owns:
        specs.append(pl.BlockSpec(own.shape, lambda i, ids: (0, 0)))
        args.append(own)
    for sets in panels:
        for p, start in zip(sets, starts):
            specs.append(
                pl.BlockSpec(
                    (1,) + p.shape[1:],
                    lambda i, ids, start=start, n=p.shape[0]: (jnp.clip(i - start, 0, n - 1), 0, 0),
                )
            )
            args.append(p)
    out_spec = pl.BlockSpec((panel, panel), lambda i, ids: (0, ids[i]))
    if old is not None:
        specs.append(out_spec)
        args.append(old)
    return pl.pallas_call(
        functools.partial(gram_kernel, counts_of, len(owns), old is not None),
        out_shape=jax.ShapeDtypeStruct((panel, features), jnp.float32),
        grid_spec=pltpu.PrefetchScalarGridSpec(
            num_scalar_prefetch=1,
            grid=(sum(counts_of),),
            in_specs=[pl.BlockSpec(memory_space=pltpu.SMEM)] + specs,
            out_specs=out_spec,
            scratch_shapes=[pltpu.VMEM(own.shape[::-1], jnp.bfloat16) for own in owns],
        ),
        input_output_aliases={} if old is None else {1 + len(args): 0},
        compiler_params=pltpu.CompilerParams(vmem_limit_bytes=VMEM_BYTES),
        cost_estimate=pl.CostEstimate(
            flops=2 * sum(o.shape[0] for o in owns) * panel * panel * sum(counts_of),
            bytes_accessed=panel * panel * 4 * sum(counts_of),
            transcendentals=0,
        ),
        interpret=INTERPRET,
    )(ids, scale, *args)


def local(tokens, routes, counts, gate_weight, up_weight):
    x, l, c = lax.axis_index("x"), lax.axis_index("l"), lax.axis_index("c")
    expert = lax.axis_index("y") * 2 + lax.axis_index("h")
    gate_panel, up_panel = gate_weight[0], up_weight[0]
    panel = gate_panel.shape[1]
    features = 16 * panel
    routed_total = jnp.sum(jnp.where(jnp.arange(8) == expert, counts, 0)).astype(jnp.float32)
    scale = (2.0 / routed_total).reshape(1)
    expert = expert.reshape(1).astype(jnp.int32)

    def member(x_of, l_of, c_of):
        return (x_of % 4) * 4 + l_of * 2 + c_of

    tagged = jnp.concatenate(
        [tokens, jnp.pad(routes.astype(tokens.dtype), ((0, 0), (0, ROUTE_LANES - 2)))], axis=1
    )
    pair = jnp.stack([tagged, swap(tagged, "l")])
    quad = jnp.stack([pair, swap(pair, "c")])
    near = ring_hop(quad, "x")
    far = ring_hop(near[0], "x")
    other = swap(near, "c")
    mine = jnp.concatenate([quad[0], near[0], other[1], far])
    mine = mine.reshape((-1, mine.shape[-1]))

    def bases(l_of, c_of):
        s = 1 - 2 * c_of
        ids = [member(x_of, l_at, c_of) for x_of in (x, x - s, x + s, x + 2) for l_at in (l_of, 1 - l_of)]
        row = jnp.repeat(12 * jnp.stack(ids), 16).astype(jnp.float32)
        return jnp.broadcast_to(row, (8, 128))

    same = (bases(l, c), bases(l, 1 - c))
    flipped = (bases(1 - l, c), bases(1 - l, 1 - c))

    def arrival(block, base):
        return [(block, base[0]), (swap(block, "c"), base[1])]

    y1 = ring_hop(mine, "y")
    z0 = far_swap(mine)
    y2 = ring_hop(y1, "y")
    z1 = far_swap(y1)
    y3 = ring_hop(y2, "y")
    z2 = far_swap(y2)
    z3 = far_swap(y3)
    a0, a1 = arrival(mine, same), arrival(y1, same)
    a2, a3 = arrival(y2, same), arrival(y3, same)
    b0, b1 = arrival(z0, flipped), arrival(z1, flipped)
    b2, b3 = arrival(z2, flipped), arrival(z3, flipped)
    chunks = [a0 + a1, b0 + a2 + a3, b1 + b2, b3]

    s = 1 - 2 * c
    ids = (
        [member(x, l_at, c_at) for c_at in (c, 1 - c) for l_at in (l, 1 - l)]
        + [member(x - s, l_at, c_at) for c_at in (c, 1 - c) for l_at in (l, 1 - l)]
        + [member(x + s, l_at, c_at) for c_at in (1 - c, c) for l_at in (l, 1 - l)]
        + [member(x + 2, l_at, c_at) for c_at in (c, 1 - c) for l_at in (l, 1 - l)]
    )
    ids = jnp.stack(ids).astype(jnp.int32)

    owns, panels = [], []
    for chunk in chunks:
        hidden = ffn(expert, chunk, gate_panel, up_panel)
        h_pair = jnp.stack([hidden, swap(hidden, "l")])
        h_quad = jnp.concatenate([h_pair, swap(h_pair, "c")])
        h_near = ring_hop(h_quad, "x")
        h_far = ring_hop(h_near[:2], "x")
        owns.append(hidden)
        panels.append([h_quad, h_near, swap(h_near, "c"), h_far, swap(h_far, "c")])

    out = gram(ids, scale, owns[:2], panels[:2], features)
    out = gram(ids, scale, owns[2:3], panels[2:3], features, out)
    out = gram(ids[:12], scale, owns[3:], [panels[3][:3]], features, out)
    out = gram(ids[12:], scale, owns[3:], [panels[3][3:]], features, out)
    return out[None]


def solution(mesh):
    fine = Mesh(mesh.devices.reshape(4, 2, 4, 2, 2), AXES)
    rows = P(AXES, None)
    weight = P(("y", "h"), None, ("x", "l", "c"))
    return jax.shard_map(
        local,
        mesh=fine,
        in_specs=(rows, rows, P(), weight, weight),
        out_specs=P(("y", "h"), ("x", "l", "c"), None),
        check_vma=False,
    )
```

time: 268 us -> 315 us (1.18)
  Pallas kernels: 0 us -> 108 us
  waiting for transfers between devices: 188 us -> 118 us
  starting transfers between devices: 0.04 us -> 64 us
  matrix products: 39 us -> 0 us
  blocking collectives: 20.8 us -> 0 us
  between operations: 14.1 us -> 1.12 us
  other arithmetic: 1.51 us -> 13.7 us
  local copies, waits for them, and re-layouts: 4.67 us -> 8.52 us
    all_gather x2 -> x0, waiting for transfers between devices: 188 us -> none  [the longest x1 131 us: local(): gram = gram_block(hidden, lax.all_gather(hidden, 'tp', axis=1, tiled=True))]
    ppermute x0 -> x44, waiting for transfers between devices: none -> 118 us  [the longest x13 69.3 us: ring_hop(): return lax.ppermute(a, (axis, 'c'), pairs)]
    pallas_call x0 -> x8, Pallas kernels: none -> 108 us  [the longest x4 67.9 us: gram(): pl.pallas_call(functools.partial(gram_kernel, counts_of, len(owns), old i...]
    ppermute x0 -> x44, starting transfers between devices: none -> 64 us  [the longest x27 36.6 us: swap(): return lax.ppermute(a, axis, [(0, 1), (1, 0)])]
    dot_general x4 -> x0, matrix products: 39 us -> none  [the longest x1 22 us: gram_block(): lax.dot_general(left_panel, right_panel, (((0,), (0,)), ((), ())), prefer...]
    all_to_all x1 -> x0, blocking collectives: 20.8 us -> none  [local(): lax.all_to_all(outgoing, 'expert', split_axis=0, concat_axis=0, tiled=True)]
    another operation x1 -> x11, other arithmetic: 0.03 us -> 8.62 us  [the longest x4 5.08 us: local(): h_pair = jnp.stack([hidden, swap(hidden, 'l')])]
    unnamed x8 -> x63, local copies, waits for them, and re-layouts: 0.02 us -> 4.59 us
  transfers between devices with their start and end apart: 2 -> 44, of which waited for: 2 -> 20; matrix products, arithmetic and copies ran while one was open for 0% -> 5% of each run, Pallas kernels for 0% -> 28%
where the time goes in v1:
time: 315 us; the launch traced here: 313 us
  waiting for transfers between devices  118 us (37%)
  Pallas kernels  108 us (34%)
  starting transfers between devices  64 us (20%)
  other arithmetic  13.7 us (4%)
  local copies, waits for them, and re-layouts  8.52 us (3%)
    ppermute x13, waiting for transfers between devices, ring_hop(): return lax.ppermute(a, (axis, 'c'), pairs)  69.3 us
    pallas_call x4, Pallas kernels, gram(): pl.pallas_call(functools.partial(gram_kernel, counts_of, len(owns), old i...  67.9 us
    pallas_call x4, Pallas kernels, ffn(): pl.pallas_call(functools.partial(ffn_kernel, slots, width, n), out_shape=...  39.7 us
    ppermute x27, starting transfers between devices, swap(): return lax.ppermute(a, axis, [(0, 1), (1, 0)])  36.6 us
    ppermute x27, waiting for transfers between devices, swap(): return lax.ppermute(a, axis, [(0, 1), (1, 0)])  26.5 us
    ppermute x4, waiting for transfers between devices, far_swap(): return lax.ppermute(a, ('h', 'l'), [(0, 3), (3, 0), (1, 2), (2, 1)])  22.1 us
    ppermute x13, starting transfers between devices, ring_hop(): return lax.ppermute(a, (axis, 'c'), pairs)  18.9 us
    ppermute x4, starting transfers between devices, far_swap(): return lax.ppermute(a, ('h', 'l'), [(0, 3), (3, 0), (1, 2), (2, 1)])  8.58 us
  transfers between devices with their start and end apart: 44, of which 20 were waited for; matrix products, arithmetic and copies ran while one was open for 5% of the time, Pallas kernels for 28%

profile of v1, /device:TPU:1, one launch (start us, length us, event | category | flops | bytes accessed | tf_op | source)
XLA Modules:
  0.0 313.0 jit_solution(17364517881216042916)
XLA Ops:
  11.9 4.9 %collective-permute-done.2 = bf16[2,2,16,3200]{3,2,1,0:T(8,128)(2,1)S(1)} collective-permute-done((bf16[2,2,16,3200]{3,2,1,0:T(8,128)(2,1)S(1)}, bf16[2,2,16,3200]{3,2,1,0:T(8,128)(2,1)S(1)}, u32[]{:S(2)}, u32[]{:S(2)}) %collective-permute-start.2) | collective-permute-done | bytes 409632 | tf_op jit(solution)/shard_map/ppermute | solution.py:19
  25.5 9.3 %collective-permute-done.5.rest_2_ = bf16[128,3200]{1,0:T(8,128)(2,1)S(1)} collective-permute-done((bf16[128,3200]{1,0:T(8,128)(2,1)S(1)}, bf16[128,3200]{1,0:T(8,128)(2,1)S(1)}, u32[]{:S(2)}, u32[]{:S(2)}) %collective-permute-start.5) | collective-permute-done | bytes 819232 | tf_op jit(solution)/shard_map/ppermute | solution.py:19
  38.6 3.6 %collective-permute-start.28 = (bf16[128,3200]{1,0:T(8,128)(2,1)S(1)}, bf16[128,3200]{1,0:T(8,128)(2,1)}, u32[]{:S(2)}, u32[]{:S(2)}) collective-permute-start(bf16[128,3200]{1,0:T(8,128)(2,1)S(1)} %bitcast.73), channel_id=1, source_target_pairs={{0,18},{18,0},{2,16},{16,2},{1,19},{19,1},{3,17},{17,3},{4,22},{22... | collective-permute-start | bytes 2457608 | tf_op jit(solution)/shard_map/ppermute | solution.py:27
  42.2 5.0 %collective-permute-done.6.rest_2_ = bf16[128,3200]{1,0:T(8,128)(2,1)S(1)} collective-permute-done((bf16[128,3200]{1,0:T(8,128)(2,1)S(1)}, bf16[128,3200]{1,0:T(8,128)(2,1)S(1)}, u32[]{:S(2)}, u32[]{:S(2)}) %collective-permute-start.6) | collective-permute-done | bytes 819232 | tf_op jit(solution)/shard_map/ppermute | solution.py:19
  47.2 3.5 %collective-permute-start.7 = (bf16[128,3200]{1,0:T(8,128)(2,1)S(1)}, bf16[128,3200]{1,0:T(8,128)(2,1)}, u32[]{:S(2)}, u32[]{:S(2)}) collective-permute-start(bf16[128,3200]{1,0:T(8,128)(2,1)S(1)} %collective-permute-done.6.rest_2_), channel_id=1, source_target_pairs={{0,32},{1,97},{32,64},{33,1},{64,96},{65,33},{96,0},{97,65},{2,34}... | collective-permute-start | bytes 2457608 | tf_op jit(solution)/shard_map/ppermute | solution.py:19
  51.0 7.7 %collective-permute-done.28.rest_0_ = bf16[128,3200]{1,0:T(8,128)(2,1)} collective-permute-done((bf16[128,3200]{1,0:T(8,128)(2,1)S(1)}, bf16[128,3200]{1,0:T(8,128)(2,1)}, u32[]{:S(2)}, u32[]{:S(2)}) %collective-permute-start.28) | collective-permute-done | bytes 819232 | tf_op jit(solution)/shard_map/ppermute | solution.py:27
  61.5 5.3 %collective-permute-start.31 = (bf16[128,3200]{1,0:T(8,128)(2,1)}, bf16[128,3200]{1,0:T(8,128)(2,1)S(1)}, u32[]{:S(2)}, u32[]{:S(2)}) collective-permute-start(bf16[128,3200]{1,0:T(8,128)(2,1)} %collective-permute-done.7.rest_4_), channel_id=1, source_target_pairs={{0,1},{1,0},{2,3},{3,2},{4,5},{5,4},{6,7},{7,6},{8,9},{9,8},{10,11... | collective-permute-start | bytes 2457608 | tf_op jit(solution)/shard_map/ppermute | solution.py:23
  69.9 12.6 %shard_map.58.rest_1_ = bf16[576,512]{1,0:T(8,128)(2,1)} custom-call(s32[1]{0:T(128)} %bitcast.5.expert_ref, f32[6,8,128]{2,1,0:T(8,128)} %copy-done.21, bf16[3072,512]{1,0:T(8,128)(2,1)} %bitcast.50, bf16[3072,512]{1,0:T(8,128)(2,1)} %bitcast.54, bf16[128,3200]{1,0:T(8,128)(2,1)} %collective-permute-done.28.rest_0_, bf16[128,3200]{1,0:T(8,128)(2,1)} %copy-done.23, ...), custom_call_target="tpu_custom_call" | custom-call | flops 3623878656 | bytes 6300000 | tf_op jit(solution)/shard_map/pallas_call | solution.py:80
  87.5 10.1 %collective-permute-done.38 = bf16[576,512]{1,0:T(8,128)(2,1)S(1)} collective-permute-done((bf16[576,512]{1,0:T(8,128)(2,1)}, bf16[576,512]{1,0:T(8,128)(2,1)S(1)}, u32[]{:S(2)}, u32[]{:S(2)}) %collective-permute-start.38) | collective-permute-done | bytes 589856 | tf_op jit(solution)/shard_map/ppermute | solution.py:23
  102.4 9.9 %shard_map.57.rest_0_ = bf16[384,512]{1,0:T(8,128)(2,1)} custom-call(s32[1]{0:T(128)} %bitcast.5.expert_ref, f32[4,8,128]{2,1,0:T(8,128)} %pad_maximum_fusion.11.base_ref, bf16[3072,512]{1,0:T(8,128)(2,1)} %bitcast.51, bf16[3072,512]{1,0:T(8,128)(2,1)} %bitcast.55, bf16[128,3200]{1,0:T(8,128)(2,1)} %bitcast.75, bf16[128,3200]{1,0:T(8,128)(2,1)} %copy-done.14, ...), custom_call_target="tpu_custom_call" | custom-call | flops 2415919104 | bytes 6300000 | tf_op jit(solution)/shard_map/pallas_call | solution.py:80
  114.2 8.7 %collective-permute-done.18.rest_2_ = bf16[128,3200]{1,0:T(8,128)(2,1)} collective-permute-done((bf16[128,3200]{1,0:T(8,128)(2,1)}, bf16[128,3200]{1,0:T(8,128)(2,1)}, u32[]{:S(2)}, u32[]{:S(2)}) %collective-permute-start.18) | collective-permute-done | bytes 819232 | tf_op jit(solution)/shard_map/ppermute | solution.py:27
  130.0 10.0 %shard_map.56.rest_0_ = bf16[384,512]{1,0:T(8,128)(2,1)} custom-call(s32[1]{0:T(128)} %bitcast.5.expert_ref, f32[4,8,128]{2,1,0:T(8,128)} %pad_maximum_fusion.10.base_ref, bf16[3072,512]{1,0:T(8,128)(2,1)} %bitcast.52, bf16[3072,512]{1,0:T(8,128)(2,1)} %bitcast.56, bf16[128,3200]{1,0:T(8,128)(2,1)} %collective-permute-done.16.rest_0_, ...), custom_call_target="tpu_custom_call" | custom-call | flops 2415919104 | bytes 6300000 | tf_op jit(solution)/shard_map/pallas_call | solution.py:80
  140.0 5.6 %collective-permute-done.8.rest_0_ = bf16[128,3200]{1,0:T(8,128)(2,1)S(1)} collective-permute-done((bf16[128,3200]{1,0:T(8,128)(2,1)}, bf16[128,3200]{1,0:T(8,128)(2,1)S(1)}, u32[]{:S(2)}, u32[]{:S(2)}) %collective-permute-start.8) | collective-permute-done | bytes 819232 | tf_op jit(solution)/shard_map/ppermute | solution.py:27
  153.3 7.3 %shard_map.55.rest_0_ = bf16[192,512]{1,0:T(8,128)(2,1)} custom-call(s32[1]{0:T(128)} %bitcast.5.expert_ref, f32[2,8,128]{2,1,0:T(8,128)} %pad_maximum_fusion.12.base_ref, bf16[3072,512]{1,0:T(8,128)(2,1)} %bitcast.53, bf16[3072,512]{1,0:T(8,128)(2,1)} %bitcast.57, bf16[128,3200]{1,0:T(8,128)(2,1)} %copy-done.13, ...), custom_call_target="tpu_custom_call" | custom-call | flops 1207959552 | bytes 6300000 | tf_op jit(solution)/shard_map/pallas_call | solution.py:80
  160.7 6.7 %collective-permute-done.10 = bf16[192,512]{1,0:T(8,128)(2,1)S(1)} collective-permute-done((bf16[192,512]{1,0:T(8,128)(2,1)}, bf16[192,512]{1,0:T(8,128)(2,1)S(1)}, u32[]{:S(2)}, u32[]{:S(2)}) %collective-permute-start.10) | collective-permute-done | bytes 196640 | tf_op jit(solution)/shard_map/ppermute | solution.py:23
  179.0 20.3 %collective-permute-done.36.rest_5_ = bf16[2,384,512]{2,1,0:T(8,128)(2,1)S(1)} collective-permute-done((bf16[2,384,512]{2,1,0:T(8,128)(2,1)S(1)}, bf16[2,384,512]{2,1,0:T(8,128)(2,1)S(1)}, u32[]{:S(2)}, u32[]{:S(2)}) %collective-permute-start.36) | collective-permute-done | bytes 786464 | tf_op jit(solution)/shard_map/ppermute | solution.py:19
  201.5 6.1 %collective-permute-done.12.rest_2_ = bf16[4,192,512]{2,1,0:T(8,128)(2,1)S(1)} collective-permute-done((bf16[4,192,512]{2,1,0:T(8,128)(2,1)S(1)}, bf16[4,192,512]{2,1,0:T(8,128)(2,1)S(1)}, u32[]{:S(2)}, u32[]{:S(2)}) %collective-permute-start.12) | collective-permute-done | bytes 786464 | tf_op jit(solution)/shard_map/ppermute | solution.py:19
  210.1 10.3 %collective-permute-done.42.rest_10_ = bf16[2,576,512]{2,1,0:T(8,128)(2,1)} collective-permute-done((bf16[2,576,512]{2,1,0:T(8,128)(2,1)S(1)}, bf16[2,576,512]{2,1,0:T(8,128)(2,1)}, u32[]{:S(2)}, u32[]{:S(2)}) %collective-permute-start.42) | collective-permute-done | bytes 1179680 | tf_op jit(solution)/shard_map/ppermute | solution.py:19
  227.6 8.2 %collective-permute-done.24.rest_4_ = bf16[2,384,512]{2,1,0:T(8,128)(2,1)} collective-permute-done((bf16[2,384,512]{2,1,0:T(8,128)(2,1)S(1)}, bf16[2,384,512]{2,1,0:T(8,128)(2,1)}, u32[]{:S(2)}, u32[]{:S(2)}) %collective-permute-start.24) | collective-permute-done | bytes 786464 | tf_op jit(solution)/shard_map/ppermute | solution.py:19
  235.8 4.4 %collective-permute-start.25 = (bf16[2,384,512]{2,1,0:T(8,128)(2,1)}, bf16[2,384,512]{2,1,0:T(8,128)(2,1)}, u32[]{:S(2)}, u32[]{:S(2)}) collective-permute-start(bf16[2,384,512]{2,1,0:T(8,128)(2,1)} %collective-permute-done.24.rest_4_), channel_id=1, source_target_pairs={{0,1},{1,0},{2,3},{3,2},{4,5},{5,4},{6,7},{7,6},{8,9},{9,8},{10,11... | collective-permute-start | bytes 2359304 | tf_op jit(solution)/shard_map/ppermute | solution.py:23
  243.3 23.9 %shard_map.59.rest_6_ = f32[512,8192]{1,0:T(8,128)} custom-call(s32[16]{0:T(128)} %stack.207.ids_ref, f32[1]{0:T(128)} %bitcast.4.scale_ref, bf16[384,512]{1,0:T(8,128)(2,1)} %shard_map.57.rest_0_, bf16[576,512]{1,0:T(8,128)(2,1)} %shard_map.58.rest_1_, bf16[4,384,512]{2,1,0:T(8,128)(2,1)} %copy-done.3, bf16[4,384,512]{2,1,0:T(8,128)(2,1)} %copy-done.7, ...), custom_call_target="tpu_custom_call" | custom-call | flops 8053063680 | bytes 16777216 | tf_op jit(solution)/shard_map/pallas_call | solution.py:157
  267.3 22.0 %shard_map.60.rest_4_ = f32[512,8192]{1,0:T(8,128)} custom-call(s32[16]{0:T(128)} %stack.207.ids_ref, f32[1]{0:T(128)} %bitcast.4.scale_ref, bf16[384,512]{1,0:T(8,128)(2,1)} %shard_map.56.rest_0_, bf16[4,384,512]{2,1,0:T(8,128)(2,1)} %copy-done.4, bf16[4,384,512]{2,1,0:T(8,128)(2,1)} %copy-done.8, ...), custom_call_target="tpu_custom_call", output_to_operand_aliasing={{}: (8, {})} | custom-call | flops 3221225472 | bytes 16777216 | tf_op jit(solution)/shard_map/pallas_call | solution.py:157
  290.2 15.8 %shard_map.61.rest_3_ = f32[512,8192]{1,0:T(8,128)} custom-call(s32[12]{0:T(128)} %stack.206.ids_ref, f32[1]{0:T(128)} %bitcast.4.scale_ref, bf16[192,512]{1,0:T(8,128)(2,1)} %shard_map.55.rest_0_, bf16[4,192,512]{2,1,0:T(8,128)(2,1)} %copy-done.9, bf16[4,192,512]{2,1,0:T(8,128)(2,1)} %copy-done.10, ...), custom_call_target="tpu_custom_call", output_to_operand_aliasing={{}: (6, {})} | custom-call | flops 1207959552 | bytes 12582912 | tf_op jit(solution)/shard_map/pallas_call | solution.py:157
  306.7 6.2 %shard_map.62 = f32[512,8192]{1,0:T(8,128)} custom-call(s32[4]{0:T(128)} %pad_add_fusion.ids_ref, f32[1]{0:T(128)} %bitcast.4.scale_ref, bf16[192,512]{1,0:T(8,128)(2,1)} %shard_map.55.rest_0_, bf16[2,192,512]{2,1,0:T(8,128)(2,1)} %copy-done.19, bf16[2,192,512]{2,1,0:T(8,128)(2,1)} %copy-done.20, ...), custom_call_target="tpu_custom_call", output_to_operand_aliasing={{}: (5, {})} | custom-call | flops 402653184 | bytes 4194304 | tf_op jit(solution)/shard_map/pallas_call | solution.py:157
  (182 shorter events, 84.4 us)
Async XLA Ops:
  38.6 20.2 %collective-permute-start.28 = (bf16[128,3200]{1,0:T(8,128)(2,1)S(1)}, bf16[128,3200]{1,0:T(8,128)(2,1)}, u32[]{:S(2)}, u32[]{:S(2)}) collective-permute-start(bf16[128,3200]{1,0:T(8,128)(2,1)S(1)} %bitcast.73), channel_id=1, source_target_pairs={{0,18},{18,0},{2,16},{16,2},{1,19},{19,1},{3,17},{17,3},{4,22},{22... | collective-permute-start | bytes 2457608 | tf_op jit(solution)/shard_map/ppermute | solution.py:27
  84.1 16.5 %collective-permute-start.26 = (bf16[128,3200]{1,0:T(8,128)(2,1)S(1)}, bf16[128,3200]{1,0:T(8,128)(2,1)S(1)}, u32[]{:S(2)}, u32[]{:S(2)}) collective-permute-start(bf16[128,3200]{1,0:T(8,128)(2,1)S(1)} %bitcast.74), channel_id=1, source_target_pairs={{0,1},{1,0},{2,3},{3,2},{4,5},{5,4},{6,7},{7,6},{8,9},{9,8},{10,11... | collective-permute-start | bytes 2457608 | tf_op jit(solution)/shard_map/ppermute | solution.py:23
  84.8 15.9 %collective-permute-start.27 = (bf16[128,3200]{1,0:T(8,128)(2,1)S(1)}, bf16[128,3200]{1,0:T(8,128)(2,1)S(1)}, u32[]{:S(2)}, u32[]{:S(2)}) collective-permute-start(bf16[128,3200]{1,0:T(8,128)(2,1)S(1)} %collective-permute-done.5.rest_2_), channel_id=1, source_target_pairs={{0,1},{1,0},{2,3},{3,2},{4,5},{5,4},{6,7},{7,6},{8,9},{9,8},{10,11... | collective-permute-start | bytes 2457608 | tf_op jit(solution)/shard_map/ppermute | solution.py:23
  84.8 29.2 %collective-permute-start.16 = (bf16[128,3200]{1,0:T(8,128)(2,1)S(1)}, bf16[128,3200]{1,0:T(8,128)(2,1)}, u32[]{:S(2)}, u32[]{:S(2)}) collective-permute-start(bf16[128,3200]{1,0:T(8,128)(2,1)S(1)} %collective-permute-done.5.rest_2_), channel_id=1, source_target_pairs={{0,18},{18,0},{2,16},{16,2},{1,19},{19,1},{3,17},{17,3},{4,22},{22... | collective-permute-start | bytes 2457608 | tf_op jit(solution)/shard_map/ppermute | solution.py:27
  87.0 35.9 %collective-permute-start.18 = (bf16[128,3200]{1,0:T(8,128)(2,1)}, bf16[128,3200]{1,0:T(8,128)(2,1)}, u32[]{:S(2)}, u32[]{:S(2)}) collective-permute-start(bf16[128,3200]{1,0:T(8,128)(2,1)} %copy-done.22), channel_id=1, source_target_pairs={{0,18},{18,0},{2,16},{16,2},{1,19},{19,1},{3,17},{17,3},{4,22},{22... | collective-permute-start | bytes 2457608 | tf_op jit(solution)/shard_map/ppermute | solution.py:27
  98.7 30.1 %collective-permute-start.39 = (bf16[2,576,512]{2,1,0:T(8,128)(2,1)S(1)}, bf16[2,576,512]{2,1,0:T(8,128)(2,1)S(1)}, u32[]{:S(2)}, u32[]{:S(2)}) collective-permute-start(bf16[2,576,512]{2,1,0:T(8,128)(2,1)S(1)} %pad_maximum_fusion.3), channel_id=1, source_target_pairs={{0,1},{1,0},{2,3},{3,2},{4,5},{5,4},{6,7},{7,6},{8,9},{9,8},{10,11... | collective-permute-start | bytes 3538952 | tf_op jit(solution)/shard_map/ppermute | solution.py:23
  113.9 16.0 %collective-permute-start.17 = (bf16[128,3200]{1,0:T(8,128)(2,1)}, bf16[128,3200]{1,0:T(8,128)(2,1)}, u32[]{:S(2)}, u32[]{:S(2)}) collective-permute-start(bf16[128,3200]{1,0:T(8,128)(2,1)} %collective-permute-done.16.rest_0_), channel_id=1, source_target_pairs={{0,1},{1,0},{2,3},{3,2},{4,5},{5,4},{6,7},{7,6},{8,9},{9,8},{10,11... | collective-permute-start | bytes 2457608 | tf_op jit(solution)/shard_map/ppermute | solution.py:23
  124.3 21.4 %collective-permute-start.8 = (bf16[128,3200]{1,0:T(8,128)(2,1)}, bf16[128,3200]{1,0:T(8,128)(2,1)S(1)}, u32[]{:S(2)}, u32[]{:S(2)}) collective-permute-start(bf16[128,3200]{1,0:T(8,128)(2,1)} %collective-permute-done.7.rest_4_), channel_id=1, source_target_pairs={{0,18},{18,0},{2,16},{16,2},{1,19},{19,1},{3,17},{17,3},{4,22},{22... | collective-permute-start | bytes 2457608 | tf_op jit(solution)/shard_map/ppermute | solution.py:27
  128.5 17.9 %collective-permute-start.33 = (bf16[2,384,512]{2,1,0:T(8,128)(2,1)}, bf16[2,384,512]{2,1,0:T(8,128)(2,1)}, u32[]{:S(2)}, u32[]{:S(2)}) collective-permute-start(bf16[2,384,512]{2,1,0:T(8,128)(2,1)} %pad_maximum_fusion.6), channel_id=1, source_target_pairs={{0,1},{1,0},{2,3},{3,2},{4,5},{5,4},{6,7},{7,6},{8,9},{9,8},{10,11... | collective-permute-start | bytes 2359304 | tf_op jit(solution)/shard_map/ppermute | solution.py:23
  129.0 46.2 %collective-permute-start.40 = (bf16[4,576,512]{2,1,0:T(8,128)(2,1)S(1)}, bf16[4,576,512]{2,1,0:T(8,128)(2,1)}, u32[]{:S(2)}, u32[]{:S(2)}) collective-permute-start(bf16[4,576,512]{2,1,0:T(8,128)(2,1)S(1)} %pad_maximum_fusion.rest_7_), channel_id=1, source_target_pairs={{0,4},{1,13},{4,8},{5,1},{8,12},{9,5},{12,0},{13,9},{2,6},{3,15},{... | collective-permute-start | bytes 7077896 | tf_op jit(solution)/shard_map/ppermute | solution.py:19
  147.7 26.3 %collective-permute-start.34 = (bf16[4,384,512]{2,1,0:T(8,128)(2,1)S(1)}, bf16[4,384,512]{2,1,0:T(8,128)(2,1)S(1)}, u32[]{:S(2)}, u32[]{:S(2)}) collective-permute-start(bf16[4,384,512]{2,1,0:T(8,128)(2,1)S(1)} %pad_maximum_fusion.2.rest_2_), channel_id=1, source_target_pairs={{0,4},{1,13},{4,8},{5,1},{8,12},{9,5},{12,0},{13,9},{2,6},{3,15},{... | collective-permute-start | bytes 4718600 | tf_op jit(solution)/shard_map/ppermute | solution.py:19
  151.8 17.4 %collective-permute-start.21 = (bf16[2,384,512]{2,1,0:T(8,128)(2,1)}, bf16[2,384,512]{2,1,0:T(8,128)(2,1)}, u32[]{:S(2)}, u32[]{:S(2)}) collective-permute-start(bf16[2,384,512]{2,1,0:T(8,128)(2,1)} %pad_maximum_fusion.5), channel_id=1, source_target_pairs={{0,1},{1,0},{2,3},{3,2},{4,5},{5,4},{6,7},{7,6},{8,9},{9,8},{10,11... | collective-permute-start | bytes 2359304 | tf_op jit(solution)/shard_map/ppermute | solution.py:23
  170.6 39.4 %collective-permute-start.22 = (bf16[4,384,512]{2,1,0:T(8,128)(2,1)S(1)}, bf16[4,384,512]{2,1,0:T(8,128)(2,1)S(1)}, u32[]{:S(2)}, u32[]{:S(2)}) collective-permute-start(bf16[4,384,512]{2,1,0:T(8,128)(2,1)S(1)} %pad_maximum_fusion.1.rest_1_), channel_id=1, source_target_pairs={{0,4},{1,13},{4,8},{5,1},{8,12},{9,5},{12,0},{13,9},{2,6},{3,15},{... | collective-permute-start | bytes 4718600 | tf_op jit(solution)/shard_map/ppermute | solution.py:19
  174.0 25.2 %collective-permute-start.36 = (bf16[2,384,512]{2,1,0:T(8,128)(2,1)S(1)}, bf16[2,384,512]{2,1,0:T(8,128)(2,1)S(1)}, u32[]{:S(2)}, u32[]{:S(2)}) collective-permute-start(bf16[2,384,512]{2,1,0:T(8,128)(2,1)S(1)} %slice.33), channel_id=1, source_target_pairs={{0,4},{1,13},{4,8},{5,1},{8,12},{9,5},{12,0},{13,9},{2,6},{3,15},{... | collective-permute-start | bytes 2359304 | tf_op jit(solution)/shard_map/ppermute | solution.py:19
  175.2 32.5 %collective-permute-start.12 = (bf16[4,192,512]{2,1,0:T(8,128)(2,1)S(1)}, bf16[4,192,512]{2,1,0:T(8,128)(2,1)S(1)}, u32[]{:S(2)}, u32[]{:S(2)}) collective-permute-start(bf16[4,192,512]{2,1,0:T(8,128)(2,1)S(1)} %pad_maximum_fusion.4.rest_1_), channel_id=1, source_target_pairs={{0,4},{1,13},{4,8},{5,1},{8,12},{9,5},{12,0},{13,9},{2,6},{3,15},{... | collective-permute-start | bytes 2359304 | tf_op jit(solution)/shard_map/ppermute | solution.py:19
  176.8 43.6 %collective-permute-start.42 = (bf16[2,576,512]{2,1,0:T(8,128)(2,1)S(1)}, bf16[2,576,512]{2,1,0:T(8,128)(2,1)}, u32[]{:S(2)}, u32[]{:S(2)}) collective-permute-start(bf16[2,576,512]{2,1,0:T(8,128)(2,1)S(1)} %slice.34), channel_id=1, source_target_pairs={{0,4},{1,13},{4,8},{5,1},{8,12},{9,5},{12,0},{13,9},{2,6},{3,15},{... | collective-permute-start | bytes 3538952 | tf_op jit(solution)/shard_map/ppermute | solution.py:19
  177.2 66.1 %collective-permute-start.41 = (bf16[4,576,512]{2,1,0:T(8,128)(2,1)}, bf16[4,576,512]{2,1,0:T(8,128)(2,1)}, u32[]{:S(2)}, u32[]{:S(2)}) collective-permute-start(bf16[4,576,512]{2,1,0:T(8,128)(2,1)} %collective-permute-done.40.rest_8_), channel_id=1, source_target_pairs={{0,1},{1,0},{2,3},{3,2},{4,5},{5,4},{6,7},{7,6},{8,9},{9,8},{10,11... | collective-permute-start | bytes 7077896 | tf_op jit(solution)/shard_map/ppermute | solution.py:23
  199.2 26.3 %collective-permute-start.37 = (bf16[2,384,512]{2,1,0:T(8,128)(2,1)S(1)}, bf16[2,384,512]{2,1,0:T(8,128)(2,1)S(1)}, u32[]{:S(2)}, u32[]{:S(2)}) collective-permute-start(bf16[2,384,512]{2,1,0:T(8,128)(2,1)S(1)} %collective-permute-done.36.rest_5_), channel_id=1, source_target_pairs={{0,1},{1,0},{2,3},{3,2},{4,5},{5,4},{6,7},{7,6},{8,9},{9,8},{10,11... | collective-permute-start | bytes 2359304 | tf_op jit(solution)/shard_map/ppermute | solution.py:23
  207.7 35.0 %collective-permute-start.35 = (bf16[4,384,512]{2,1,0:T(8,128)(2,1)S(1)}, bf16[4,384,512]{2,1,0:T(8,128)(2,1)}, u32[]{:S(2)}, u32[]{:S(2)}) collective-permute-start(bf16[4,384,512]{2,1,0:T(8,128)(2,1)S(1)} %collective-permute-done.34.rest_3_), channel_id=1, source_target_pairs={{0,1},{1,0},{2,3},{3,2},{4,5},{5,4},{6,7},{7,6},{8,9},{9,8},{10,11... | collective-permute-start | bytes 4718600 | tf_op jit(solution)/shard_map/ppermute | solution.py:23
  220.4 22.4 %collective-permute-start.43 = (bf16[2,576,512]{2,1,0:T(8,128)(2,1)}, bf16[2,576,512]{2,1,0:T(8,128)(2,1)}, u32[]{:S(2)}, u32[]{:S(2)}) collective-permute-start(bf16[2,576,512]{2,1,0:T(8,128)(2,1)} %collective-permute-done.42.rest_10_), channel_id=1, source_target_pairs={{0,1},{1,0},{2,3},{3,2},{4,5},{5,4},{6,7},{7,6},{8,9},{9,8},{10,11... | collective-permute-start | bytes 3538952 | tf_op jit(solution)/shard_map/ppermute | solution.py:23
  225.6 41.7 %collective-permute-start.23 = (bf16[4,384,512]{2,1,0:T(8,128)(2,1)S(1)}, bf16[4,384,512]{2,1,0:T(8,128)(2,1)}, u32[]{:S(2)}, u32[]{:S(2)}) collective-permute-start(bf16[4,384,512]{2,1,0:T(8,128)(2,1)S(1)} %collective-permute-done.22.rest_2_), channel_id=1, source_target_pairs={{0,1},{1,0},{2,3},{3,2},{4,5},{5,4},{6,7},{7,6},{8,9},{9,8},{10,11... | collective-permute-start | bytes 4718600 | tf_op jit(solution)/shard_map/ppermute | solution.py:23
  235.8 31.5 %collective-permute-start.25 = (bf16[2,384,512]{2,1,0:T(8,128)(2,1)}, bf16[2,384,512]{2,1,0:T(8,128)(2,1)}, u32[]{:S(2)}, u32[]{:S(2)}) collective-permute-start(bf16[2,384,512]{2,1,0:T(8,128)(2,1)} %collective-permute-done.24.rest_4_), channel_id=1, source_target_pairs={{0,1},{1,0},{2,3},{3,2},{4,5},{5,4},{6,7},{7,6},{8,9},{9,8},{10,11... | collective-permute-start | bytes 2359304 | tf_op jit(solution)/shard_map/ppermute | solution.py:23
  242.7 46.5 %collective-permute-start.15 = (bf16[4,192,512]{2,1,0:T(8,128)(2,1)}, bf16[4,192,512]{2,1,0:T(8,128)(2,1)S(1)}, u32[]{:S(2)}, u32[]{:S(2)}) collective-permute-start(bf16[4,192,512]{2,1,0:T(8,128)(2,1)} %copy-done.10), channel_id=1, source_target_pairs={{0,1},{1,0},{2,3},{3,2},{4,5},{5,4},{6,7},{7,6},{8,9},{9,8},{10,11... | collective-permute-start | bytes 2359304 | tf_op jit(solution)/shard_map/ppermute | solution.py:23
  242.8 63.1 %collective-permute-start.14 = (bf16[2,192,512]{2,1,0:T(8,128)(2,1)}, bf16[2,192,512]{2,1,0:T(8,128)(2,1)S(1)}, u32[]{:S(2)}, u32[]{:S(2)}) collective-permute-start(bf16[2,192,512]{2,1,0:T(8,128)(2,1)} %copy-done.19), channel_id=1, source_target_pairs={{0,1},{1,0},{2,3},{3,2},{4,5},{5,4},{6,7},{7,6},{8,9},{9,8},{10,11... | collective-permute-start | bytes 1179656 | tf_op jit(solution)/shard_map/ppermute | solution.py:23
  (47 other events, 659.5 us)
